TPU v7x, 128 devices: a whole 4x4x4 slice. The times are simulated.
128 devices in a mesh: section: 8 (over x_lo, y), tensor: 16 (over z, x_hi, core).
Axes of the slice: x: 4 (x_hi: 2, x_lo: 2; x = x_hi * 2 + x_lo), y: 4, z: 4, core: 2. Of those that a mesh axis runs over, the one named last changes fastest.
Arguments:
- hidden: bfloat16 [512, 4096], P('section', 'tensor'), may hold values from -24 to 24
- weight: bfloat16 [131072, 4096], P(('section', 'tensor')), may hold values from -1 to 1
- targets: int32 [512], replicated, may hold values from 0 to 131071
- loss_grad: float32 [512], replicated, may hold values from 4 to 16
Outputs:
- token_loss: float32 [512], replicated
- grad_hidden: bfloat16 [512, 4096], P('section', 'tensor')
- grad_weight: bfloat16 [131072, 4096], P(('section', 'tensor'))
All inputs are finite; a program needn't handle non-finite values.
Results may differ from a plain program's by a relative error of at most 0.0047.
Values may be sent and summed in bfloat16 or wider, within the bound.
A program may use at most 64 MiB of HBM per device.

v0:
```python
import jax
import jax.numpy as jnp
from jax import lax
from jax.sharding import PartitionSpec as P


def shards(hidden, weight, targets, loss_grad):
    vocab_rows = weight.shape[0]
    vocab_start = (
        lax.axis_index("section") * lax.axis_size("tensor") + lax.axis_index("tensor")
    ) * vocab_rows
    feature_block = lax.all_gather(hidden, "tensor", axis=1, tiled=True)
    gathered = lax.all_gather(feature_block, "section", axis=0, tiled=True)
    logits = lax.dot_general(
        gathered, weight, (((1,), (1,)), ((), ())), preferred_element_type=jnp.float32
    )
    columns = jnp.arange(vocab_rows, dtype=jnp.int32)
    target_mask = columns[None, :] == (targets - vocab_start)[:, None]
    picked_part = jnp.sum(jnp.where(target_mask, logits, jnp.float32(0.0)), axis=1)
    local_max = jnp.max(logits, axis=1)
    row_max = lax.pmax(local_max, ("section", "tensor"))
    shifted = jnp.exp(logits - row_max[:, None])
    row_total, picked = lax.psum((jnp.sum(shifted, axis=1), picked_part), ("section", "tensor"))
    token_loss = row_max + jnp.log(row_total) - picked
    grad_logits = (
        loss_grad[:, None] * (shifted / row_total[:, None] - target_mask.astype(jnp.float32))
    ).astype(jnp.bfloat16)
    grad_weight = lax.dot_general(
        grad_logits, gathered, (((0,), (0,)), ((), ())), preferred_element_type=jnp.float32
    ).astype(jnp.bfloat16)
    full_term = jnp.dot(grad_logits, weight, preferred_element_type=jnp.float32)
    feature_sums = lax.psum_scatter(full_term, "tensor", scatter_dimension=1, tiled=True)
    grad_hidden = lax.psum_scatter(feature_sums, "section", scatter_dimension=0, tiled=True)
    return (token_loss, grad_hidden.astype(jnp.bfloat16), grad_weight)


def solution(mesh):
    return jax.shard_map(
        shards,
        mesh=mesh,
        in_specs=(P("section", "tensor"), P(("section", "tensor"), None), P(), P()),
        out_specs=(P(), P("section", "tensor"), P(("section", "tensor"), None)),
        check_vma=False,
    )
```

profile of v0, /device:TPU:0, one launch (start us, length us, event | category | flops | bytes accessed | tf_op | source)
XLA Modules:
  0.0 379.6 jit_solution(8945495457731537896)
XLA Ops:
  7.2 0.0 all-gather.2.cloned.1.call-start
  7.2 29.2 %all_gather.6 = bf16[64,4096]{1,0:T(8,128)(2,1)} all-gather(bf16[64,256]{1,0:T(8,128)(2,1)} %param.4), channel_id=1, replica_groups=mesh['section'=8,'tensor'=16] {'tensor'}, dimensions={1}, use_global_device_ids=true | all-gather | bytes 557056 | tf_op jit(solution)/shard_map/all_gather | solution.py:12
  36.5 0.0 all-gather.2.cloned.1.call-update
  36.5 0.0 reduce-scatter.3.cloned.1.call-start
  36.5 0.7 broadcast_subtract_fusion
  37.2 48.5 %all-gather.2.cloned.1.call-done = bf16[512,4096]{1,0:T(8,128)(2,1)} async-done(((bf16[64,4096]{1,0:T(8,128)(2,1)}), bf16[512,4096]{1,0:T(8,128)(2,1)}) %all-gather.2.cloned.1.call-update) | async-done | bytes 4194320 | tf_op jit(solution)/shard_map/all_gather | solution.py:13
  85.7 8.4 %fusion.2 = (f32[512]{0:T(512)S(1)}, f32[512,1024]{1,0:T(8,128)S(1)}) fusion(bf16[512,4096]{1,0:T(8,128)(2,1)} %all-gather.2.cloned.1.call-done, bf16[1024,4096]{1,0:T(8,128)(2,1)} %param.5), kind=kOutput, calls=%fused_computation.9 | convolution fusion | flops 4295491072 | bytes 14682112 | tf_op jit(solution)/shard_map/dot_general | solution.py:14
  94.1 0.0 copy-start
  94.1 64.5 %pmax.7 = f32[512]{0:T(512)S(1)} all-reduce(f32[512]{0:T(512)S(1)} %get-tuple-element.7), channel_id=1, replica_groups=mesh['section'=8,'tensor'=16] {'section','tensor'}, use_global_device_ids=true, to_apply=%region_1.2 | all-reduce | flops 512 | bytes 4096 | tf_op jit(solution)/shard_map/pmax | solution.py:21
  158.6 0.6 fusion
  159.2 63.9 %all-reduce = (f32[512]{0:T(512)S(1)}, f32[512]{0:T(512)S(1)}) all-reduce(f32[512]{0:T(512)S(1)} %get-tuple-element.4, f32[512]{0:T(512)S(1)} %get-tuple-element.3), channel_id=1, replica_groups=mesh['section'=8,'tensor'=16] {'section','tensor'}, use_global_device_ids=true, to_apply=%region_5.6 | all-reduce | flops 1024 | bytes 8192 | tf_op jit(solution)/shard_map/psum | solution.py:23
  223.1 0.0 copy-done
  223.1 10.8 %fusion.1 = f32[512,4096]{1,0:T(8,128)} fusion(bf16[1024,4096]{1,0:T(8,128)(2,1)} %param.5, f32[512,1024]{1,0:T(8,128)S(1)} %get-tuple-element.8, f32[512]{0:T(512)S(1)} %get-tuple-element.6, f32[512]{0:T(512)S(1)} %copy-done, s32[512]{0:T(512)S(1)} %broadcast_subtract_fusion, f32[512]{0:T(512)S(1)} %pmax.7), kind=kOutput, calls=%fused_computation.8 | convolution fusion | flops 4298637312 | bytes 18882560 | tf_op jit(solution)/shard_map/dot_general | solution.py:31
  233.9 0.0 reduce-scatter.3.cloned.1.call-update
  233.9 0.0 reduce-scatter.5.cloned.1.call-start
  234.0 0.6 add_subtract_fusion
  234.6 98.1 %reduce-scatter.3.cloned.1.call-done = f32[512,256]{1,0:T(8,128)} async-done(((f32[512,4096]{1,0:T(8,128)}), f32[512,256]{1,0:T(8,128)}) %reduce-scatter.3.cloned.1.call-update) | async-done | bytes 524304 | tf_op jit(solution)/shard_map/reduce_scatter | solution.py:32
  332.7 0.0 reduce-scatter.5.cloned.1.call-update
  332.7 9.5 %convolution_convert_fusion = bf16[1024,4096]{1,0:T(8,128)(2,1)} fusion(bf16[512,4096]{1,0:T(8,128)(2,1)} %all-gather.2.cloned.1.call-done, f32[512,1024]{1,0:T(8,128)S(1)} %get-tuple-element.8, f32[512]{0:T(512)S(1)} %get-tuple-element.6, f32[512]{0:T(512)S(1)} %copy-done, s32[512]{0:T(512)S(1)} %broadcast_subtract_fusion, f32[512]{0:T(512)S(1)} %pmax.7), kind=kOutput, calls=%fused_computation | convolution fusion | flops 4302831616 | bytes 14688256 | tf_op jit(solution)/shard_map/dot_general | solution.py:28
  342.2 29.3 %reduce-scatter.5.cloned.1.call-done = f32[64,256]{1,0:T(8,128)} async-done(((f32[512,256]{1,0:T(8,128)}), f32[64,256]{1,0:T(8,128)}) %reduce-scatter.5.cloned.1.call-update) | async-done | bytes 65552 | tf_op jit(solution)/shard_map/reduce_scatter | solution.py:33
  371.6 1.5 convert_element_type.14
Async XLA Ops:
  7.2 78.6 %all-gather.2.cloned.1.call-start = ((), (), s32[]{:S(2)}) async-start(), calls=%async_computation.2 | async-start | bytes 4718592 | tf_op jit(solution)/shard_map/all_gather | solution.py:13
  36.5 296.2 %reduce-scatter.3.cloned.1.call-start = ((), (), s32[]{:S(2)}) async-start(), calls=%async_computation.3 | async-start | bytes 8912896 | tf_op jit(solution)/shard_map/reduce_scatter | solution.py:32
  94.1 129.0 %copy-start = (f32[512]{0:T(512)S(1)}, f32[512]{0:T(512)}, u32[]{:S(2)}) copy-start(f32[512]{0:T(512)} %param.7) | copy-start | bytes 6148
  233.9 137.6 %reduce-scatter.5.cloned.1.call-start = ((), (), s32[]{:S(2)}) async-start(), calls=%async_computation.4 | async-start | bytes 589824 | tf_op jit(solution)/shard_map/reduce_scatter | solution.py:33
Sparse Core Ops, SparseCore 0:
  36.6 49.0 all-gather.1
  234.1 98.5 reduce-scatter.2
  335.0 36.4 reduce-scatter.4
where the time goes:
time: 380 us
  waiting for transfers between devices  176 us (46%)
  blocking collectives  158 us (42%)
  matrix products  28.7 us (8%)
  between operations  13.8 us (4%)
    reduce_scatter x1, waiting for transfers between devices, shards(): lax.psum_scatter(full_term, 'tensor', scatter_dimension=1, tiled=True)  98.1 us
    pmax x1, blocking collectives, shards(): row_max = lax.pmax(local_max, ('section', 'tensor'))  64.5 us
    psum x1, blocking collectives, shards(): lax.psum((jnp.sum(shifted, axis=1), picked_part), ('section', 'tensor'))  63.9 us
    all_gather x1, waiting for transfers between devices, shards(): gathered = lax.all_gather(feature_block, 'section', axis=0, tiled=True)  48.5 us
    reduce_scatter x1, waiting for transfers between devices, shards(): lax.psum_scatter(feature_sums, 'section', scatter_dimension=0, tiled=True)  29.3 us
    all_gather x1, blocking collectives, shards(): feature_block = lax.all_gather(hidden, 'tensor', axis=1, tiled=True)  29.2 us
    dot_general x1, matrix products, shards(): full_term = jnp.dot(grad_logits, weight, preferred_element_type=jnp.float32)  10.8 us
    dot_general x1, matrix products, shards(): lax.dot_general(grad_logits, gathered, (((0,), (0,)), ((), ())), preferre...  9.54 us
  transfers between devices with their start and end apart: 3, of which 3 were waited for; matrix products, arithmetic and copies ran while one was open for 3% of the time, Pallas kernels for 0%

commit v1 on v0

v1 whole, which is shorter than its diff:
```python
import jax
import jax.numpy as jnp
from jax import lax
from jax.experimental import pallas as pl
from jax.experimental.pallas import tpu as pltpu
from jax.sharding import PartitionSpec as P

MESH = pl.DeviceIdType.MESH
F32, BF16 = jnp.float32, jnp.bfloat16

ORDERS = ((0, 1, 2), (1, 2, 0), (2, 0, 1))
ROWS = ((0, 48), (48, 48), (96, 32))


def place():
    s, t = lax.axis_index("section"), lax.axis_index("tensor")
    return ((t // 2) % 2) * 2 + s // 4, s % 4, t // 4, t % 2


def device(x, y, z, c):
    return ((x % 2) * 4 + y, z * 4 + (x // 2) * 2 + c)


def region(at, rows=None):
    x, y, z = at
    whole = slice(None)
    ix = (
        whole if x is None else x % 2,
        whole if y is None else y,
        whole if z is None else z,
        whole if x is None else x // 2,
    )
    return ix if rows is None else ix + (pl.ds(rows[0], rows[1]),)


def moved(at, axis, delta):
    at = list(at)
    at[axis] = (at[axis] + delta) % 4
    return tuple(at)


def combine(parts):
    top = jnp.max(parts[:, 0], axis=0)
    total = jnp.sum(parts[:, 1] * jnp.exp(parts[:, 0] - top[None]), axis=0)
    return top, total, jnp.sum(parts[:, 2], axis=0)


def flat(rows):
    return jnp.concatenate([rows[i : i + 1] for i in range(4)], axis=1)


def kernel(
    hid_ref, w_hbm, tgt_ref, lg_ref,
    loss_ref, gh_ref, gw_ref,
    w, g, lt, glt, gl, own, give, take, r,
    rx1, ry1, rz1, rx2, ry2, rz2, r3a, r3b, r3c,
    st_core, st_plane, st_axis,
    w_sem, ag_s, ag_r, rel_s, rel_r, core_s, core_r, rs_s, rs_r,
    sc_s, sc_r, sp_s, sp_r, sa_s, sa_r,
):
    x, y, z, c = place()
    me = (x, y, z)
    vocab, depth = w.shape
    tokens = lt.shape[1]
    partner = device(x, y, z, 1 - c)

    load_w = pltpu.make_async_copy(w_hbm, w, w_sem)
    load_w.start()

    own_g = (c,) + region(me)
    g[own_g + (pl.ds(0, 64),)] = hid_ref[:, 0:128]
    g[own_g + (pl.ds(64, 64),)] = hid_ref[:, 128:256]

    barrier = pltpu.get_barrier_semaphore()
    peers = [partner]
    for dx in range(4):
        for dy in range(4):
            if dx or dy:
                peers.append(device((x + dx) % 4, (y + dy) % 4, z, c))
    for dz in range(1, 4):
        peers.append(device(x, y, (z + dz) % 4, c))
    for peer in peers:
        pl.semaphore_signal(barrier, inc=1, device_id=peer, device_id_type=MESH)
    pl.semaphore_wait(barrier, len(peers))

    sends = {}
    relays = []

    def send(k, p, d):
        axis = ORDERS[k][p]
        at = tuple(None if a in ORDERS[k][:p] else me[a] for a in range(3))
        ref = g.at[(c,) + region(at, ROWS[k])]
        i = (k * 3 + p) * 3 + d - 1
        cp = pltpu.make_async_remote_copy(
            ref, ref, ag_s.at[i], ag_r.at[i],
            device_id=device(*moved(me, axis, d), c), device_id_type=MESH,
        )
        cp.start()
        sends[k, p, d] = cp

    def relay(k, d):
        axis = ORDERS[k][2]
        at = tuple((me[a] - d) % 4 if a == axis else None for a in range(3))
        ref = g.at[(c,) + region(at, ROWS[k])]
        i = k * 4 + d
        cp = pltpu.make_async_remote_copy(
            ref, ref, rel_s.at[i], rel_r.at[i], device_id=partner, device_id_type=MESH
        )
        cp.start()
        relays.append(cp)

    for k in range(3):
        for d in (1, 3, 2):
            send(k, 0, d)
    for p in (1, 2):
        for k in range(3):
            for d in (1, 3, 2):
                sends[k, p - 1, d].wait_recv()
            for d in (1, 3, 2):
                send(k, p, d)
    for k in range(3):
        relay(k, 0)
    for d in (1, 3, 2):
        for k in range(3):
            sends[k, 2, d].wait_recv()
            relay(k, d)
    for cp in relays:
        cp.wait_recv()
    load_w.wait()

    def features(q):
        zz, xx = q // 2, q % 2
        parts = [
            g[cc, :, :, zz, xx, pl.ds(64 * h, 64), :].reshape(tokens, 128)
            for cc in range(2)
            for h in range(2)
        ]
        return jnp.concatenate(parts, axis=1)

    def columns(q, width=512):
        return pl.ds(pl.multiple_of(q * width, width), width)

    lt[...] = jnp.zeros_like(lt)

    def logit_step(q, _):
        rhs = features(q)
        for i in range(4):
            rows = pl.ds(i * (vocab // 4), vocab // 4)
            lt[rows, :] += lax.dot_general(
                w[rows, columns(q)], rhs, (((1,), (1,)), ((), ())),
                preferred_element_type=F32,
            )
        return 0

    lax.fori_loop(0, 8, logit_step, 0)

    s_idx, t_idx = lax.axis_index("section"), lax.axis_index("tensor")
    local = tgt_ref[...] - (s_idx * 16 + t_idx) * vocab
    chunk = 64
    n_chunks = vocab // chunk

    def hit(i):
        ids = lax.broadcasted_iota(jnp.int32, (chunk, tokens), 0) + i * chunk
        return ids == local

    def max_step(i, top):
        return jnp.maximum(top, lt[pl.ds(pl.multiple_of(i * chunk, chunk), chunk), :])

    top = lax.fori_loop(1, n_chunks, max_step, lt[pl.ds(0, chunk), :])
    top = jnp.max(top, axis=0, keepdims=True)

    def exp_step(i, carry):
        total, picked = carry
        rows = pl.ds(pl.multiple_of(i * chunk, chunk), chunk)
        value = lt[rows, :]
        e = jnp.exp(value - top)
        lt[rows, :] = e
        picked = picked + jnp.sum(jnp.where(hit(i), value, 0.0), axis=0, keepdims=True)
        return total + jnp.sum(e, axis=0, keepdims=True), picked

    zero = jnp.zeros((1, tokens), F32)
    total, picked = lax.fori_loop(0, n_chunks, exp_step, (zero, zero))

    for j, v in enumerate((top, total, picked)):
        for i in range(4):
            st_core[0, j, i : i + 1, :] = v[:, 128 * i : 128 * (i + 1)]
    core_copy = pltpu.make_async_remote_copy(
        st_core.at[0], st_core.at[1], sc_s, sc_r, device_id=partner, device_id_type=MESH
    )
    core_copy.start()
    core_copy.wait_recv()
    for j, v in enumerate(combine(st_core[...])):
        st_plane[0, j] = v
    plane_copies = []
    for dx in range(4):
        for dy in range(4):
            i = dx * 4 + dy
            if i:
                cp = pltpu.make_async_remote_copy(
                    st_plane.at[0], st_plane.at[i], sp_s.at[i], sp_r.at[i],
                    device_id=device((x + dx) % 4, (y + dy) % 4, z, c),
                    device_id_type=MESH,
                )
                cp.start()
                plane_copies.append(cp)
    for cp in plane_copies:
        cp.wait_recv()
    for j, v in enumerate(combine(st_plane[...])):
        st_axis[0, j] = v
    axis_copies = []
    for d in (1, 3, 2):
        cp = pltpu.make_async_remote_copy(
            st_axis.at[0], st_axis.at[d], sa_s.at[d], sa_r.at[d],
            device_id=device(x, y, (z + d) % 4, c), device_id_type=MESH,
        )
        cp.start()
        axis_copies.append(cp)
    for cp in axis_copies:
        cp.wait_recv()
    m_all, s_all, p_all = combine(st_axis[...])
    loss_ref[...] = m_all + jnp.log(s_all) - p_all
    lg = lg_ref[...]
    scale = lg * jnp.exp(top - flat(m_all)) / flat(s_all)

    def grad_step(i, _):
        rows = pl.ds(pl.multiple_of(i * chunk, chunk), chunk)
        value = lt[rows, :] * scale - jnp.where(hit(i), lg, 0.0)
        glt[rows, :] = value.astype(BF16)
        return 0

    lax.fori_loop(0, n_chunks, grad_step, 0)
    for i in range(8):
        gl[:, 128 * i : 128 * (i + 1)] = glt[128 * i : 128 * (i + 1), :].T

    def term(t):
        return jnp.dot(gl[...], w[:, columns(t, 256)], preferred_element_type=F32)

    def core_send(q):
        zz, xx = q // 2, q % 2
        return pltpu.make_async_remote_copy(
            give.at[q], take.at[q], core_s.at[q], core_r.at[q],
            device_id=partner, device_id_type=MESH,
        )

    def join(q):
        zz, xx = q // 2, q % 2
        core_send(q).wait_recv()
        r[:, :, zz, xx] = (own[q].astype(F32) + take[q].astype(F32)).astype(BF16)

    def term_step(q, _):
        value = term(q * 2 + 1 - c).astype(BF16)
        give[q, :, :, 0:64] = value[:, 0:128].reshape(2, 4, 64, 128)
        give[q, :, :, 64:128] = value[:, 128:256].reshape(2, 4, 64, 128)
        core_send(q).start()
        value = term(q * 2 + c)
        own[q, :, :, 0:64] = value[:, 0:128].reshape(2, 4, 64, 128)
        own[q, :, :, 64:128] = value[:, 128:256].reshape(2, 4, 64, 128)
        pl.when(q > 0)(lambda: join(q - 1))
        return 0

    lax.fori_loop(0, 8, term_step, 0)
    join(7)

    slots = ((rz1, ry2, r3a), (rx1, rz2, r3b), (ry1, rx2, r3c))
    rs = {}

    def rs_send(k, p):
        axis = ORDERS[k][2 - p]
        for d in (1, 3, 2):
            at = tuple(
                (me[a] + d) % 4 if a == axis else None if a in ORDERS[k][: 2 - p] else me[a]
                for a in range(3)
            )
            i = (k * 3 + p) * 3 + d - 1
            cp = pltpu.make_async_remote_copy(
                r.at[region(at, ROWS[k])], slots[k][p].at[d - 1], rs_s.at[i], rs_r.at[i],
                device_id=device(*moved(me, axis, d), c), device_id_type=MESH,
            )
            cp.start()
            rs[k, p, d] = cp

    def rs_sum(k, p):
        axis = ORDERS[k][2 - p]
        at = tuple(None if a in ORDERS[k][: 2 - p] else me[a] for a in range(3))
        ix = region(at, ROWS[k])
        value = r[ix].astype(F32)
        for d in (1, 3, 2):
            rs[k, p, d].wait_recv()
            value = value + slots[k][p][d - 1].astype(F32)
        r[ix] = value.astype(BF16)

    def weight_step(q, _):
        gw_ref[:, columns(q)] = jnp.dot(
            glt[...], features(q), preferred_element_type=F32
        ).astype(BF16)
        return 0

    for k in range(3):
        rs_send(k, 0)
    lax.fori_loop(0, 4, weight_step, 0)
    for k in range(3):
        rs_sum(k, 0)
        rs_send(k, 1)
    lax.fori_loop(4, 6, weight_step, 0)
    for k in range(3):
        rs_sum(k, 1)
        rs_send(k, 2)
    lax.fori_loop(6, 8, weight_step, 0)
    for k in range(3):
        rs_sum(k, 2)
    mine = region(me)
    gh_ref[:, 0:128] = r[mine + (pl.ds(0, 64),)]
    gh_ref[:, 128:256] = r[mine + (pl.ds(64, 64),)]

    for cp in (
        list(sends.values()) + relays + [core_copy] + plane_copies + axis_copies + list(rs.values())
    ):
        cp.wait_send()

    def drain(q, _):
        core_send(q).wait_send()
        return 0

    lax.fori_loop(0, 8, drain, 0)


def write_kernel(src, dst, sem):
    cp = pltpu.make_async_copy(src, dst, sem)
    cp.start()
    cp.wait()


def shards(hidden, weight, targets, loss_grad):
    vocab, depth = weight.shape
    tokens = targets.shape[0]
    dma = pltpu.SemaphoreType.DMA
    vmem = pl.BlockSpec(memory_space=pltpu.VMEM)
    slot = lambda *s: pltpu.VMEM((3,) + s + (128,), BF16)
    loss, grad_hidden, grad_weight = pl.pallas_call(
        kernel,
        out_shape=(
            jax.ShapeDtypeStruct((4, 128), F32),
            jax.ShapeDtypeStruct(hidden.shape, BF16),
            pltpu.VMEM((vocab, depth), BF16),
        ),
        in_specs=[vmem, pl.BlockSpec(memory_space=pl.ANY), vmem, vmem],
        out_specs=(vmem, vmem, vmem),
        scratch_shapes=[
            pltpu.VMEM((vocab, depth), BF16),
            pltpu.VMEM((2, 2, 4, 4, 2, 128, 128), BF16),
            pltpu.VMEM((vocab, tokens), F32),
            pltpu.VMEM((vocab, tokens), BF16),
            pltpu.VMEM((tokens, vocab), BF16),
            pltpu.VMEM((8, 2, 4, 128, 128), F32),
            pltpu.VMEM((8, 2, 4, 128, 128), BF16),
            pltpu.VMEM((8, 2, 4, 128, 128), BF16),
            pltpu.VMEM((2, 4, 4, 2, 128, 128), BF16),
            slot(4, 4, 48), slot(2, 4, 2, 32), slot(2, 4, 2, 48),
            slot(4, 32), slot(2, 2, 48), slot(4, 48),
            slot(48), slot(48), slot(32),
            pltpu.VMEM((2, 3, 4, 128), F32),
            pltpu.VMEM((16, 3, 4, 128), F32),
            pltpu.VMEM((4, 3, 4, 128), F32),
            dma,
            dma((27,)), dma((27,)), dma((12,)), dma((12,)),
            dma((8,)), dma((8,)), dma((27,)), dma((27,)),
            dma, dma, dma((16,)), dma((16,)), dma((4,)), dma((4,)),
        ],
        compiler_params=pltpu.CompilerParams(
            collective_id=0, has_side_effects=True, vmem_limit_bytes=50 * 2**20
        ),
    )(hidden, weight, targets.reshape(1, tokens), loss_grad.reshape(1, tokens))
    grad_weight = pl.pallas_call(
        write_kernel,
        out_shape=jax.ShapeDtypeStruct((vocab, depth), BF16),
        in_specs=[vmem],
        out_specs=pl.BlockSpec(memory_space=pl.ANY),
        scratch_shapes=[dma],
        compiler_params=pltpu.CompilerParams(vmem_limit_bytes=16 * 2**20),
    )(grad_weight)
    return loss.reshape(tokens), grad_hidden, grad_weight


def solution(mesh):
    return jax.shard_map(
        shards,
        mesh=mesh,
        in_specs=(P("section", "tensor"), P(("section", "tensor"), None), P(), P()),
        out_specs=(P(), P("section", "tensor"), P(("section", "tensor"), None)),
        check_vma=False,
    )
```

time: 380 us -> 86.4 us (0.23)
  waiting for transfers between devices: 176 us -> 0 us
  blocking collectives: 158 us -> 0 us
  Pallas kernels: 0 us -> 84.4 us
  matrix products: 28.7 us -> 0 us
  between operations: 13.8 us -> 0.67 us
    reduce_scatter x2 -> x0, waiting for transfers between devices: 127 us -> none  [the longest x1 98.1 us: shards(): lax.psum_scatter(full_term, 'tensor', scatter_dimension=1, tiled=True)]
    pallas_call x0 -> x2, Pallas kernels: none -> 84.4 us  [the longest x1 81 us: shards(): pl.pallas_call(kernel, out_shape=(jax.ShapeDtypeStruct((4, 128), F32), ja...]
    pmax x1 -> x0, blocking collectives: 64.5 us -> none  [shards(): row_max = lax.pmax(local_max, ('section', 'tensor'))]
    psum x1 -> x0, blocking collectives: 63.9 us -> none  [shards(): lax.psum((jnp.sum(shifted, axis=1), picked_part), ('section', 'tensor'))]
    all_gather x1 -> x0, waiting for transfers between devices: 48.5 us -> none  [shards(): gathered = lax.all_gather(feature_block, 'section', axis=0, tiled=True)]
    all_gather x1 -> x0, blocking collectives: 29.2 us -> none  [shards(): feature_block = lax.all_gather(hidden, 'tensor', axis=1, tiled=True)]
    dot_general x3 -> x0, matrix products: 28.7 us -> none  [the longest x1 10.8 us: shards(): full_term = jnp.dot(grad_logits, weight, preferred_element_type=jnp.float32)]
  transfers between devices with their start and end apart: 3 -> 0, of which waited for: 3 -> 0; matrix products, arithmetic and copies ran while one was open for 3% -> 0% of each run, Pallas kernels for 0% -> 0%
where the time goes in v1:
time: 86.4 us; the launch traced here: 86.3 us
  Pallas kernels  84.4 us (98%)
  local copies, waits for them, and re-layouts  1.2 us (1%)
    pallas_call x1, Pallas kernels, shards(): pl.pallas_call(kernel, out_shape=(jax.ShapeDtypeStruct((4, 128), F32), ja...  81 us
    pallas_call x1, Pallas kernels, shards(): pl.pallas_call(write_kernel, out_shape=jax.ShapeDtypeStruct((vocab, depth...  3.41 us

profile of v1, /device:TPU:0, one launch (start us, length us, event | category | flops | bytes accessed | tf_op | source)
XLA Modules:
  0.0 86.3 jit_solution(4414516977301228399)
XLA Ops:
  0.6 81.0 %shard_map.67 = (f32[4,128]{1,0:T(4,128)}, bf16[64,256]{1,0:T(8,128)(2,1)}, bf16[1024,4096]{1,0:T(8,128)(2,1)S(1)}) custom-call(bf16[64,256]{1,0:T(8,128)(2,1)} %hid_ref.1, bf16[1024,4096]{1,0:T(8,128)(2,1)} %w_hbm.1, s32[1,512]{1,0:T(1,128)} %bitcast.4, f32[1,512]{1,0:T(1,128)} %bitcast.5), custom_call_target="tpu_custom_call" | custom-call | tf_op jit(solution)/shard_map/pallas_call | solution.py:339
  81.6 0.0 copy-start.1
  81.6 0.0 copy-start
  81.6 3.4 %shard_map.68 = bf16[1024,4096]{1,0:T(8,128)(2,1)} custom-call(bf16[1024,4096]{1,0:T(8,128)(2,1)S(1)} %get-tuple-element.8.src), custom_call_target="tpu_custom_call" | custom-call | tf_op jit(solution)/shard_map/pallas_call | solution.py:373
  85.1 0.0 copy-done.1
  85.1 0.6 copy.9
  85.6 0.0 copy-done
  85.7 0.6 copy.10
Async XLA Ops:
  81.6 3.4 %copy-start.1 = (f32[4,128]{1,0:T(4,128)S(1)}, f32[4,128]{1,0:T(4,128)}, u32[]{:S(2)}) copy-start(f32[4,128]{1,0:T(4,128)} %get-tuple-element.6) | copy-start | bytes 6148
  81.6 4.0 %copy-start = (bf16[64,256]{1,0:T(8,128)(2,1)S(1)}, bf16[64,256]{1,0:T(8,128)(2,1)}, u32[]{:S(2)}) copy-start(bf16[64,256]{1,0:T(8,128)(2,1)} %get-tuple-element.13) | copy-start | bytes 98308

commit v2 on v0

v2 whole, which is shorter than its diff:
```python
import jax
import jax.numpy as jnp
from jax import lax
from jax.experimental import pallas as pl
from jax.experimental.pallas import tpu as pltpu
from jax.sharding import PartitionSpec as P

MESH = pl.DeviceIdType.MESH
F32, BF16 = jnp.float32, jnp.bfloat16
X, Y, Z = 0, 1, 2

ORDERS = ((X, Y, Z), (Y, Z, X), (X, Z, Y))
ROWS = ((0, 32), (32, 48), (80, 48))
NEAR = (1, 3, 2)
COPIES = 134


def place():
    s, t = lax.axis_index("section"), lax.axis_index("tensor")
    return ((t // 2) % 2) * 2 + s // 4, s % 4, t // 4, t % 2


def device(x, y, z, c):
    return ((x % 2) * 4 + y, z * 4 + (x // 2) * 2 + c)


def region(at, rows=None):
    x, y, z = at
    whole = slice(None)
    ix = (
        whole if x is None else x % 2,
        whole if y is None else y,
        whole if z is None else z,
        whole if x is None else x // 2,
    )
    return ix if rows is None else ix + (pl.ds(rows[0], rows[1]),)


def combine(parts):
    top = jnp.max(parts[:, 0], axis=0)
    total = jnp.sum(parts[:, 1] * jnp.exp(parts[:, 0] - top[None]), axis=0)
    return top, total, jnp.sum(parts[:, 2], axis=0)


def flat(rows):
    return jnp.concatenate([rows[i : i + 1] for i in range(4)], axis=1)


def kernel(
    hid_ref, w_hbm, tgt_ref, lg_ref,
    loss_ref, gh_ref, gw_ref,
    w, g, lt, glt, gl, own, give, take, r,
    a0, b0, c0, a1, b1, c1, a2, b2, c2, fa, fb, fc,
    st_core, st_plane, st_axis,
    w_sem, send_sem, recv_sem,
):
    x, y, z, c = place()
    me = (x, y, z)
    vocab, depth = w.shape
    tokens = lt.shape[1]
    partner = device(x, y, z, 1 - c)

    load_w = pltpu.make_async_copy(w_hbm, w, w_sem)
    load_w.start()

    own_g = (c,) + region(me)
    g[own_g + (pl.ds(0, 64),)] = hid_ref[:, 0:128]
    g[own_g + (pl.ds(64, 64),)] = hid_ref[:, 128:256]

    barrier = pltpu.get_barrier_semaphore()
    peers = [partner]
    for dx in range(4):
        for dy in range(4):
            if dx or dy:
                peers.append(device((x + dx) % 4, (y + dy) % 4, z, c))
    for dz in range(1, 4):
        peers.append(device(x, y, (z + dz) % 4, c))
    for peer in peers:
        pl.semaphore_signal(barrier, inc=1, device_id=peer, device_id_type=MESH)
    lt[...] = jnp.zeros_like(lt)
    pl.semaphore_wait(barrier, len(peers))

    copies = []

    def send(src, dst, to):
        i = len(copies)
        cp = pltpu.make_async_remote_copy(
            src, dst, send_sem.at[i], recv_sem.at[i], device_id=to, device_id_type=MESH
        )
        cp.start()
        copies.append(cp)
        return cp

    def peer(axis, d):
        return device(*[(me[a] + d) % 4 if a == axis else me[a] for a in range(3)], c)

    def spot(k, **at):
        out = [None, None, None]
        for name, axis in zip(("first", "second", "last"), ORDERS[k]):
            d = at.get(name, 0)
            out[axis] = None if d == "all" else (me[axis] + d) % 4
        return tuple(out)

    def spread(k, role, d, **at):
        ref = g.at[(c,) + region(spot(k, **at), ROWS[k])]
        return send(ref, ref, peer(ORDERS[k][role], d))

    got0, got1, got2 = {}, {}, {}
    for k in range(3):
        for d in NEAR:
            got0[k, d] = spread(k, 0, d)
    for k in range(3):
        for d in NEAR:
            got0[k, d].wait_recv()
        for d in NEAR:
            got1[k, d] = spread(k, 1, d, first="all")
    for k in range(3):
        for d in NEAR:
            got2[k, 0, d] = spread(k, 2, d, first="all")
    for s in NEAR:
        for k in range(3):
            got1[k, s].wait_recv()
            for d in NEAR:
                got2[k, s, d] = spread(k, 2, d, first="all", second=-s)

    def relay(s):
        done = []
        for k in range(3):
            if k == 0:
                if s:
                    for i in (0,) + NEAR:
                        got2[0, i, s].wait_recv()
            else:
                for d in NEAR:
                    got2[k, s, d].wait_recv()
            ref = g.at[(c,) + region((None, None, (z - s) % 4), ROWS[k])]
            done.append(send(ref, ref, partner))
        return done

    def features(zz):
        parts = [
            g[cc, :, :, zz, xx, pl.ds(64 * h, 64), :].reshape(tokens, 128)
            for xx in range(2)
            for cc in range(2)
            for h in range(2)
        ]
        return jnp.concatenate(parts, axis=1)

    def columns(i, width):
        return pl.ds(pl.multiple_of(i * width, width), width)

    def logits(s):
        zz = (z - s) % 4

        def step(i, _):
            rows = columns(i, 256)
            lt[rows, :] += lax.dot_general(
                w[rows, columns(zz, 1024)], features(zz), (((1,), (1,)), ((), ())),
                preferred_element_type=F32,
            )
            return 0

        lax.fori_loop(0, vocab // 256, step, 0)

    relayed = relay(0)
    load_w.wait()
    before = 0
    for s in NEAR:
        upcoming = relay(s)
        for cp in relayed:
            cp.wait_recv()
        logits(before)
        relayed, before = upcoming, s
    for cp in relayed:
        cp.wait_recv()
    logits(before)

    s_idx, t_idx = lax.axis_index("section"), lax.axis_index("tensor")
    local = tgt_ref[...] - (s_idx * 16 + t_idx) * vocab
    chunk = 64
    n_chunks = vocab // chunk

    def hit(i):
        ids = lax.broadcasted_iota(jnp.int32, (chunk, tokens), 0) + i * chunk
        return ids == local

    def max_step(i, top):
        return jnp.maximum(top, lt[pl.ds(pl.multiple_of(i * chunk, chunk), chunk), :])

    top = lax.fori_loop(1, n_chunks, max_step, lt[pl.ds(0, chunk), :])
    top = jnp.max(top, axis=0, keepdims=True)

    def exp_step(i, carry):
        total, picked = carry
        rows = pl.ds(pl.multiple_of(i * chunk, chunk), chunk)
        value = lt[rows, :]
        e = jnp.exp(value - top)
        lt[rows, :] = e
        picked = picked + jnp.sum(jnp.where(hit(i), value, 0.0), axis=0, keepdims=True)
        return total + jnp.sum(e, axis=0, keepdims=True), picked

    zero = jnp.zeros((1, tokens), F32)
    total, picked = lax.fori_loop(0, n_chunks, exp_step, (zero, zero))

    for j, v in enumerate((top, total, picked)):
        for i in range(4):
            st_core[0, j, i : i + 1, :] = v[:, 128 * i : 128 * (i + 1)]
    send(st_core.at[0], st_core.at[1], partner).wait_recv()
    for j, v in enumerate(combine(st_core[...])):
        st_plane[0, j] = v
    joined = []
    for dx in range(4):
        for dy in range(4):
            i = dx * 4 + dy
            if i:
                to = device((x + dx) % 4, (y + dy) % 4, z, c)
                joined.append(send(st_plane.at[0], st_plane.at[i], to))
    for cp in joined:
        cp.wait_recv()
    for j, v in enumerate(combine(st_plane[...])):
        st_axis[0, j] = v
    joined = [send(st_axis.at[0], st_axis.at[d], peer(Z, d)) for d in NEAR]
    for cp in joined:
        cp.wait_recv()
    m_all, s_all, p_all = combine(st_axis[...])
    loss_ref[...] = m_all + jnp.log(s_all) - p_all
    lg = lg_ref[...]
    scale = lg * jnp.exp(top - flat(m_all)) / flat(s_all)

    def grad_step(i, _):
        rows = pl.ds(pl.multiple_of(i * chunk, chunk), chunk)
        value = lt[rows, :] * scale - jnp.where(hit(i), lg, 0.0)
        glt[rows, :] = value.astype(BF16)
        return 0

    lax.fori_loop(0, n_chunks, grad_step, 0)
    for i in range(8):
        gl[:, 128 * i : 128 * (i + 1)] = glt[128 * i : 128 * (i + 1), :].T

    def term(zz, xx, cc, out):
        t = (zz * 2 + xx) * 2 + cc
        value = jnp.dot(gl[...], w[:, columns(t, 256)], preferred_element_type=F32)
        value = value.astype(out.dtype)
        out[xx, :, :, 0:64] = value[:, 0:128].reshape(2, 4, 64, 128)
        out[xx, :, :, 64:128] = value[:, 128:256].reshape(2, 4, 64, 128)

    def both(zz, cc, out):
        def step(xx, _):
            term(zz, xx, cc, out)
            return 0

        lax.fori_loop(0, 2, step, 0)

    def swap(i, s):
        both((z + s) % 4, 1 - c, give.at[i])
        return send(give.at[i], take.at[i], partner)

    slots0, slots1, slots2 = (a0, b0, c0), (a1, b1, c1), (a2, b2, c2)
    finals = (fa, fb, fc)
    red0, red1, red2 = {}, {}, {}

    def reduce_z(s):
        if s:
            ref = r.at[region(spot(0, first="all", second="all", last=s), ROWS[0])]
            red0[0, s] = send(ref, a0.at[s - 1], peer(Z, s))
        for k in (1, 2):
            for d in NEAR:
                ref = r.at[region(spot(k, first="all", second=s, last=d), ROWS[k])]
                red0[k, s, d] = send(ref, slots0[k].at[s, d - 1], peer(ORDERS[k][2], d))

    def line(k, s):
        ix = region(spot(k, first="all", second=s), ROWS[k])
        value = r[ix].astype(F32)
        for d in NEAR:
            if k == 0:
                value = value + a0[d - 1, :, (y + s) % 4].astype(F32)
            else:
                red0[k, s, d].wait_recv()
                value = value + slots0[k][s, d - 1].astype(F32)
        return ix, value

    def pass_line(k, s):
        ix, value = line(k, s)
        r[ix] = value.astype(BF16)
        red1[k, s] = send(r.at[ix], slots1[k].at[s - 1], peer(ORDERS[k][1], s))

    def own_line(k):
        value = line(k, 0)[1]
        for d in NEAR:
            red1[k, d].wait_recv()
            value = value + slots1[k][d - 1].astype(F32)
        finals[k][...] = value
        axis = ORDERS[k][0]
        for d in NEAR:
            n = (me[axis] + d) % 4
            ref = finals[k].at[(n % 2, n // 2) if axis == X else (n,)]
            red2[k, d] = send(ref, slots2[k].at[d - 1], peer(axis, d))

    def weight_grad(start, stop):
        def step(i, _):
            for h in range(2):
                rows = slice(512 * h, 512 * (h + 1))
                gw_ref[rows, columns(i, 1024)] = jnp.dot(
                    glt[rows, :], features(i), preferred_element_type=F32
                ).astype(BF16)
            return 0

        lax.fori_loop(start, stop, step, 0)

    turns = NEAR + (0,)
    swaps = [swap(0, turns[0])]
    for i, s in enumerate(turns):
        if i < 3:
            swaps.append(swap(i + 1, turns[i + 1]))
        both((z + s) % 4, c, own)
        swaps[i].wait_recv()
        for xx in range(2):
            r[:, :, (z + s) % 4, xx] = (own[xx] + take[i, xx].astype(F32)).astype(BF16)
        reduce_z(s)
    weight_grad(0, 1)
    for k in (1, 2):
        pass_line(k, 1)
    weight_grad(1, 2)
    for k in (1, 2):
        pass_line(k, 3)
    weight_grad(2, 3)
    for d in NEAR:
        red0[0, d].wait_recv()
    for s in NEAR:
        pass_line(0, s)
    for k in (1, 2):
        pass_line(k, 2)
    weight_grad(3, 4)
    for k in range(3):
        own_line(k)
    mine = region(me)
    for k in range(3):
        axis = ORDERS[k][0]
        n = me[axis]
        value = finals[k][(n % 2, n // 2) if axis == X else (n,)]
        for d in NEAR:
            red2[k, d].wait_recv()
            value = value + slots2[k][d - 1]
        r[region(me, ROWS[k])] = value.astype(BF16)
    gh_ref[:, 0:128] = r[mine + (pl.ds(0, 64),)]
    gh_ref[:, 128:256] = r[mine + (pl.ds(64, 64),)]

    assert len(copies) == COPIES, len(copies)
    for cp in copies:
        cp.wait_send()


def write_kernel(gw, loss, gh, gw_out, loss_out, gh_out, sem):
    pairs = ((gw, gw_out), (loss, loss_out), (gh, gh_out))
    copies = [pltpu.make_async_copy(a, b, sem.at[i]) for i, (a, b) in enumerate(pairs)]
    for cp in copies:
        cp.start()
    for cp in copies:
        cp.wait()


def shards(hidden, weight, targets, loss_grad):
    vocab, depth = weight.shape
    tokens = targets.shape[0]
    dma = pltpu.SemaphoreType.DMA
    vmem = pl.BlockSpec(memory_space=pltpu.VMEM)
    anywhere = pl.BlockSpec(memory_space=pl.ANY)
    slot = lambda *s, t=BF16: pltpu.VMEM(s + (128,), t)
    loss, grad_hidden, grad_weight = pl.pallas_call(
        kernel,
        out_shape=(
            pltpu.VMEM((4, 128), F32),
            pltpu.VMEM(hidden.shape, BF16),
            pltpu.VMEM((vocab, depth), BF16),
        ),
        in_specs=[vmem, anywhere, vmem, vmem],
        out_specs=(vmem, vmem, vmem),
        scratch_shapes=[
            pltpu.VMEM((vocab, depth), BF16),
            pltpu.VMEM((2, 2, 4, 4, 2, 128, 128), BF16),
            pltpu.VMEM((vocab, tokens), F32),
            pltpu.VMEM((vocab, tokens), BF16),
            pltpu.VMEM((tokens, vocab), BF16),
            pltpu.VMEM((2, 2, 4, 128, 128), F32),
            pltpu.VMEM((4, 2, 2, 4, 128, 128), BF16),
            pltpu.VMEM((4, 2, 2, 4, 128, 128), BF16),
            pltpu.VMEM((2, 4, 4, 2, 128, 128), BF16),
            slot(3, 2, 4, 2, 32), slot(4, 3, 4, 48), slot(4, 3, 2, 2, 48),
            slot(3, 2, 2, 32), slot(3, 4, 48), slot(3, 2, 2, 48),
            slot(3, 32, t=F32), slot(3, 48, t=F32), slot(3, 48, t=F32),
            slot(2, 2, 32, t=F32), slot(4, 48, t=F32), slot(2, 2, 48, t=F32),
            pltpu.VMEM((2, 3, 4, 128), F32),
            pltpu.VMEM((16, 3, 4, 128), F32),
            pltpu.VMEM((4, 3, 4, 128), F32),
            dma, dma((COPIES,)), dma((COPIES,)),
        ],
        compiler_params=pltpu.CompilerParams(
            collective_id=0, has_side_effects=True, vmem_limit_bytes=48 * 2**20
        ),
    )(hidden, weight, targets.reshape(1, tokens), loss_grad.reshape(1, tokens))
    grad_weight, loss, grad_hidden = pl.pallas_call(
        write_kernel,
        out_shape=(
            jax.ShapeDtypeStruct((vocab, depth), BF16),
            jax.ShapeDtypeStruct((4, 128), F32),
            jax.ShapeDtypeStruct(hidden.shape, BF16),
        ),
        in_specs=[vmem] * 3,
        out_specs=(anywhere,) * 3,
        scratch_shapes=[dma((3,))],
        compiler_params=pltpu.CompilerParams(vmem_limit_bytes=16 * 2**20),
    )(grad_weight, loss, grad_hidden)
    return loss.reshape(tokens), grad_hidden, grad_weight


def solution(mesh):
    return jax.shard_map(
        shards,
        mesh=mesh,
        in_specs=(P("section", "tensor"), P(("section", "tensor"), None), P(), P()),
        out_specs=(P(), P("section", "tensor"), P(("section", "tensor"), None)),
        check_vma=False,
    )
```

time: 380 us -> 71.1 us (0.19)
  waiting for transfers between devices: 176 us -> 0 us
  blocking collectives: 158 us -> 0 us
  Pallas kernels: 0 us -> 70.2 us
  matrix products: 28.7 us -> 0 us
  between operations: 13.8 us -> 0.64 us
    reduce_scatter x2 -> x0, waiting for transfers between devices: 127 us -> none  [the longest x1 98.1 us: shards(): lax.psum_scatter(full_term, 'tensor', scatter_dimension=1, tiled=True)]
    pallas_call x0 -> x2, Pallas kernels: none -> 70.2 us  [the longest x1 66.8 us: shards(): pl.pallas_call(kernel, out_shape=(pltpu.VMEM((4, 128), F32), pltpu.VMEM(h...]
    pmax x1 -> x0, blocking collectives: 64.5 us -> none  [shards(): row_max = lax.pmax(local_max, ('section', 'tensor'))]
    psum x1 -> x0, blocking collectives: 63.9 us -> none  [shards(): lax.psum((jnp.sum(shifted, axis=1), picked_part), ('section', 'tensor'))]
    all_gather x1 -> x0, waiting for transfers between devices: 48.5 us -> none  [shards(): gathered = lax.all_gather(feature_block, 'section', axis=0, tiled=True)]
    all_gather x1 -> x0, blocking collectives: 29.2 us -> none  [shards(): feature_block = lax.all_gather(hidden, 'tensor', axis=1, tiled=True)]
    dot_general x3 -> x0, matrix products: 28.7 us -> none  [the longest x1 10.8 us: shards(): full_term = jnp.dot(grad_logits, weight, preferred_element_type=jnp.float32)]
  transfers between devices with their start and end apart: 3 -> 0, of which waited for: 3 -> 0; matrix products, arithmetic and copies ran while one was open for 3% -> 0% of each run, Pallas kernels for 0% -> 0%
where the time goes in v2:
time: 71.1 us; the launch traced here: 70.9 us
  Pallas kernels  70.2 us (99%)
    pallas_call x1, Pallas kernels, shards(): pl.pallas_call(kernel, out_shape=(pltpu.VMEM((4, 128), F32), pltpu.VMEM(h...  66.8 us
    pallas_call x1, Pallas kernels, shards(): pl.pallas_call(write_kernel, out_shape=(jax.ShapeDtypeStruct((vocab, dept...  3.43 us

profile of v2, /device:TPU:0, one launch (start us, length us, event | category | flops | bytes accessed | tf_op | source)
XLA Modules:
  0.0 70.9 jit_solution(7299139735919482030)
XLA Ops:
  0.6 66.8 %shard_map.67 = (f32[4,128]{1,0:T(4,128)S(1)}, bf16[64,256]{1,0:T(8,128)(2,1)S(1)}, bf16[1024,4096]{1,0:T(8,128)(2,1)S(1)}) custom-call(bf16[64,256]{1,0:T(8,128)(2,1)} %hid_ref.1, bf16[1024,4096]{1,0:T(8,128)(2,1)} %w_hbm.1, s32[1,512]{1,0:T(1,128)} %bitcast.3, f32[1,512]{1,0:T(1,128)} %bitcast.4), custom_call_target="tpu_custom_call" | custom-call | tf_op jit(solution)/shard_map/pallas_call | solution.py:369
  67.5 3.4 %shard_map.68 = (bf16[1024,4096]{1,0:T(8,128)(2,1)}, f32[4,128]{1,0:T(4,128)}, bf16[64,256]{1,0:T(8,128)(2,1)}) custom-call(bf16[1024,4096]{1,0:T(8,128)(2,1)S(1)} %get-tuple-element.9.gw, f32[4,128]{1,0:T(4,128)S(1)} %get-tuple-element.10.loss, bf16[64,256]{1,0:T(8,128)(2,1)S(1)} %get-tuple-element.11.gh), custom_call_target="tpu_custom_call" | custom-call | tf_op jit(solution)/shard_map/pallas_call | solution.py:401

commit v3 on v2

--- a/solution.py
+++ b/solution.py
@@ -12,7 +12,8 @@
 ORDERS = ((X, Y, Z), (Y, Z, X), (X, Z, Y))
 ROWS = ((0, 32), (32, 48), (80, 48))
 NEAR = (1, 3, 2)
-COPIES = 134
+COPIES = 191
+PIECES = 8
 
 
 def place():
@@ -50,8 +51,8 @@
     hid_ref, w_hbm, tgt_ref, lg_ref,
     loss_ref, gh_ref, gw_ref,
     w, g, lt, glt, gl, own, give, take, r,
-    a0, b0, c0, a1, b1, c1, a2, b2, c2, fa, fb, fc,
-    st_core, st_plane, st_axis,
+    a0, b0, c0, a1, b1, c1, fa, fb, fc,
+    st_plane, st_axis,
     w_sem, send_sem, recv_sem,
 ):
     x, y, z, c = place()
@@ -60,6 +61,9 @@
     tokens = lt.shape[1]
     partner = device(x, y, z, 1 - c)
 
+    def there(moves, cc=c):
+        return device(*[(me[a] + moves.get(a, 0)) % 4 for a in range(3)], cc)
+
     load_w = pltpu.make_async_copy(w_hbm, w, w_sem)
     load_w.start()
 
@@ -69,14 +73,11 @@
 
     barrier = pltpu.get_barrier_semaphore()
     peers = [partner]
-    for dx in range(4):
-        for dy in range(4):
-            if dx or dy:
-                peers.append(device((x + dx) % 4, (y + dy) % 4, z, c))
-    for dz in range(1, 4):
-        peers.append(device(x, y, (z + dz) % 4, c))
-    for peer in peers:
-        pl.semaphore_signal(barrier, inc=1, device_id=peer, device_id_type=MESH)
+    for d in NEAR:
+        peers += [there({axis: d}) for axis in (X, Y, Z)] + [there({Z: d}, 1 - c)]
+        peers += [there({p: d, q: e}) for p, q in ((X, Y), (Y, Z), (X, Z)) for e in NEAR]
+    for to in peers:
+        pl.semaphore_signal(barrier, inc=1, device_id=to, device_id_type=MESH)
     lt[...] = jnp.zeros_like(lt)
     pl.semaphore_wait(barrier, len(peers))
 
@@ -91,9 +92,6 @@
         copies.append(cp)
         return cp
 
-    def peer(axis, d):
-        return device(*[(me[a] + d) % 4 if a == axis else me[a] for a in range(3)], c)
-
     def spot(k, **at):
         out = [None, None, None]
         for name, axis in zip(("first", "second", "last"), ORDERS[k]):
@@ -101,27 +99,23 @@
             out[axis] = None if d == "all" else (me[axis] + d) % 4
         return tuple(out)
 
-    def spread(k, role, d, **at):
+    def spread(k, to, **at):
         ref = g.at[(c,) + region(spot(k, **at), ROWS[k])]
-        return send(ref, ref, peer(ORDERS[k][role], d))
-
-    got0, got1, got2 = {}, {}, {}
-    for k in range(3):
-        for d in NEAR:
-            got0[k, d] = spread(k, 0, d)
-    for k in range(3):
-        for d in NEAR:
-            got0[k, d].wait_recv()
-        for d in NEAR:
-            got1[k, d] = spread(k, 1, d, first="all")
-    for k in range(3):
-        for d in NEAR:
-            got2[k, 0, d] = spread(k, 2, d, first="all")
-    for s in NEAR:
+        return send(ref, ref, to)
+
+    got1, got2 = {}, {}
+    for s in (0,) + NEAR:
         for k in range(3):
-            got1[k, s].wait_recv()
+            for d in (0,) + NEAR:
+                if s or d:
+                    got1[k, s, d] = spread(k, there({ORDERS[k][0]: d, ORDERS[k][1]: s}))
+    for s in (0,) + NEAR:
+        for k in range(3):
+            for d in (0,) + NEAR:
+                if s or d:
+                    got1[k, s, d].wait_recv()
             for d in NEAR:
-                got2[k, s, d] = spread(k, 2, d, first="all", second=-s)
+                got2[k, s, d] = spread(k, there({ORDERS[k][2]: d}), first="all", second=-s)
 
     def relay(s):
         done = []
@@ -137,11 +131,11 @@
             done.append(send(ref, ref, partner))
         return done
 
-    def features(zz):
+    def features(zz, classes=(0, 1)):
         parts = [
             g[cc, :, :, zz, xx, pl.ds(64 * h, 64), :].reshape(tokens, 128)
             for xx in range(2)
-            for cc in range(2)
+            for cc in classes
             for h in range(2)
         ]
         return jnp.concatenate(parts, axis=1)
@@ -149,31 +143,34 @@
     def columns(i, width):
         return pl.ds(pl.multiple_of(i * width, width), width)
 
-    def logits(s):
+    def logits(s, cc=None):
         zz = (z - s) % 4
-
-        def step(i, _):
-            rows = columns(i, 256)
-            lt[rows, :] += lax.dot_general(
-                w[rows, columns(zz, 1024)], features(zz), (((1,), (1,)), ((), ())),
-                preferred_element_type=F32,
-            )
-            return 0
-
-        lax.fori_loop(0, vocab // 256, step, 0)
-
-    relayed = relay(0)
-    load_w.wait()
-    before = 0
-    for s in NEAR:
-        upcoming = relay(s)
+        if cc is None:
+            part, rhs = w[:, columns(zz, 1024)], features(zz)
+        else:
+            part = jnp.concatenate([w[:, columns((zz * 2 + xx) * 2 + cc, 256)] for xx in range(2)], axis=1)
+            rhs = features(zz, (cc,))
+        lt[...] += lax.dot_general(
+            part, rhs, (((1,), (1,)), ((), ())), preferred_element_type=F32
+        )
+
+    def arrived(relayed):
         for cp in relayed:
             cp.wait_recv()
-        logits(before)
-        relayed, before = upcoming, s
-    for cp in relayed:
-        cp.wait_recv()
-    logits(before)
+
+    relayed = {0: relay(0)}
+    load_w.wait()
+    arrived(relayed[0])
+    logits(0)
+    for s in NEAR:
+        relayed[s] = relay(s)
+    logits(1, c)
+    arrived(relayed[1])
+    logits(1, 1 - c)
+    arrived(relayed[3])
+    logits(3)
+    arrived(relayed[2])
+    logits(2)
 
     s_idx, t_idx = lax.axis_index("section"), lax.axis_index("tensor")
     local = tgt_ref[...] - (s_idx * 16 + t_idx) * vocab
@@ -204,22 +201,23 @@
 
     for j, v in enumerate((top, total, picked)):
         for i in range(4):
-            st_core[0, j, i : i + 1, :] = v[:, 128 * i : 128 * (i + 1)]
-    send(st_core.at[0], st_core.at[1], partner).wait_recv()
-    for j, v in enumerate(combine(st_core[...])):
-        st_plane[0, j] = v
+            st_plane[0, j, i : i + 1, :] = v[:, 128 * i : 128 * (i + 1)]
     joined = []
     for dx in range(4):
         for dy in range(4):
             i = dx * 4 + dy
             if i:
-                to = device((x + dx) % 4, (y + dy) % 4, z, c)
-                joined.append(send(st_plane.at[0], st_plane.at[i], to))
+                joined.append(send(st_plane.at[0], st_plane.at[i], there({X: dx, Y: dy})))
     for cp in joined:
         cp.wait_recv()
     for j, v in enumerate(combine(st_plane[...])):
         st_axis[0, j] = v
-    joined = [send(st_axis.at[0], st_axis.at[d], peer(Z, d)) for d in NEAR]
+    joined = [
+        send(st_axis.at[0], st_axis.at[d * 2 + i], there({Z: d}, cc))
+        for i, cc in enumerate((c, 1 - c))
+        for d in (0,) + NEAR
+        if d or i
+    ]
     for cp in joined:
         cp.wait_recv()
     m_all, s_all, p_all = combine(st_axis[...])
@@ -255,18 +253,18 @@
         both((z + s) % 4, 1 - c, give.at[i])
         return send(give.at[i], take.at[i], partner)
 
-    slots0, slots1, slots2 = (a0, b0, c0), (a1, b1, c1), (a2, b2, c2)
+    slots0, slots1 = (a0, b0, c0), (a1, b1, c1)
     finals = (fa, fb, fc)
-    red0, red1, red2 = {}, {}, {}
+    red0, red1 = {}, {}
 
     def reduce_z(s):
         if s:
             ref = r.at[region(spot(0, first="all", second="all", last=s), ROWS[0])]
-            red0[0, s] = send(ref, a0.at[s - 1], peer(Z, s))
+            red0[0, s] = send(ref, a0.at[s - 1], there({Z: s}))
         for k in (1, 2):
             for d in NEAR:
                 ref = r.at[region(spot(k, first="all", second=s, last=d), ROWS[k])]
-                red0[k, s, d] = send(ref, slots0[k].at[s, d - 1], peer(ORDERS[k][2], d))
+                red0[k, s, d] = send(ref, slots0[k].at[s, d - 1], there({ORDERS[k][2]: d}))
 
     def line(k, s):
         ix = region(spot(k, first="all", second=s), ROWS[k])
@@ -282,19 +280,13 @@
     def pass_line(k, s):
         ix, value = line(k, s)
         r[ix] = value.astype(BF16)
-        red1[k, s] = send(r.at[ix], slots1[k].at[s - 1], peer(ORDERS[k][1], s))
-
-    def own_line(k):
-        value = line(k, 0)[1]
-        for d in NEAR:
-            red1[k, d].wait_recv()
-            value = value + slots1[k][d - 1].astype(F32)
-        finals[k][...] = value
-        axis = ORDERS[k][0]
-        for d in NEAR:
-            n = (me[axis] + d) % 4
-            ref = finals[k].at[(n % 2, n // 2) if axis == X else (n,)]
-            red2[k, d] = send(ref, slots2[k].at[d - 1], peer(axis, d))
+        if s == 0:
+            finals[k][...] = value
+        for d in NEAR + (0,):
+            if s or d:
+                ref = r.at[region(spot(k, first=d, second=s), ROWS[k])]
+                to = there({ORDERS[k][0]: d, ORDERS[k][1]: s})
+                red1[k, s, d] = send(ref, slots1[k].at[s * 4 + d], to)
 
     def weight_grad(start, stop):
         def step(i, _):
@@ -328,19 +320,21 @@
         red0[0, d].wait_recv()
     for s in NEAR:
         pass_line(0, s)
+    pass_line(0, 0)
     for k in (1, 2):
         pass_line(k, 2)
+    for k in (1, 2):
+        pass_line(k, 0)
     weight_grad(3, 4)
-    for k in range(3):
-        own_line(k)
     mine = region(me)
     for k in range(3):
         axis = ORDERS[k][0]
         n = me[axis]
         value = finals[k][(n % 2, n // 2) if axis == X else (n,)]
-        for d in NEAR:
-            red2[k, d].wait_recv()
-            value = value + slots2[k][d - 1]
+        for (kk, s, d), cp in red1.items():
+            if kk == k:
+                cp.wait_recv()
+                value = value + slots1[k][s * 4 + d].astype(F32)
         r[region(me, ROWS[k])] = value.astype(BF16)
     gh_ref[:, 0:128] = r[mine + (pl.ds(0, 64),)]
     gh_ref[:, 128:256] = r[mine + (pl.ds(64, 64),)]
@@ -351,7 +345,9 @@
 
 
 def write_kernel(gw, loss, gh, gw_out, loss_out, gh_out, sem):
-    pairs = ((gw, gw_out), (loss, loss_out), (gh, gh_out))
+    step = gw.shape[0] // PIECES
+    pairs = [(gw.at[pl.ds(i * step, step)], gw_out.at[pl.ds(i * step, step)]) for i in range(PIECES)]
+    pairs += [(loss, loss_out), (gh, gh_out)]
     copies = [pltpu.make_async_copy(a, b, sem.at[i]) for i, (a, b) in enumerate(pairs)]
     for cp in copies:
         cp.start()
@@ -386,12 +382,10 @@
             pltpu.VMEM((4, 2, 2, 4, 128, 128), BF16),
             pltpu.VMEM((2, 4, 4, 2, 128, 128), BF16),
             slot(3, 2, 4, 2, 32), slot(4, 3, 4, 48), slot(4, 3, 2, 2, 48),
-            slot(3, 2, 2, 32), slot(3, 4, 48), slot(3, 2, 2, 48),
-            slot(3, 32, t=F32), slot(3, 48, t=F32), slot(3, 48, t=F32),
+            slot(16, 32), slot(16, 48), slot(16, 48),
             slot(2, 2, 32, t=F32), slot(4, 48, t=F32), slot(2, 2, 48, t=F32),
-            pltpu.VMEM((2, 3, 4, 128), F32),
             pltpu.VMEM((16, 3, 4, 128), F32),
-            pltpu.VMEM((4, 3, 4, 128), F32),
+            pltpu.VMEM((8, 3, 4, 128), F32),
             dma, dma((COPIES,)), dma((COPIES,)),
         ],
         compiler_params=pltpu.CompilerParams(
@@ -407,7 +401,7 @@
         ),
         in_specs=[vmem] * 3,
         out_specs=(anywhere,) * 3,
-        scratch_shapes=[dma((3,))],
+        scratch_shapes=[dma((PIECES + 2,))],
         compiler_params=pltpu.CompilerParams(vmem_limit_bytes=16 * 2**20),
     )(grad_weight, loss, grad_hidden)
     return loss.reshape(tokens), grad_hidden, grad_weight

time: 71.1 us -> 63.8 us (0.90)
  Pallas kernels: 70.2 us -> 62.8 us
    pallas_call x1, Pallas kernels: 66.8 us -> 59.4 us  [shards(): pl.pallas_call(kernel, out_shape=(pltpu.VMEM((4, 128), F32), pltpu.VMEM(h...]
where the time goes in v3:
time: 63.8 us; the launch traced here: 63.6 us
  Pallas kernels  62.8 us (98%)
  between operations  0.8 us (1%)
    pallas_call x1, Pallas kernels, shards(): pl.pallas_call(kernel, out_shape=(pltpu.VMEM((4, 128), F32), pltpu.VMEM(h...  59.4 us
    pallas_call x1, Pallas kernels, shards(): pl.pallas_call(write_kernel, out_shape=(jax.ShapeDtypeStruct((vocab, dept...  3.39 us

profile of v3, /device:TPU:0, one launch (start us, length us, event | category | flops | bytes accessed | tf_op | source)
XLA Modules:
  0.0 63.6 jit_solution(2042479539119085028)
XLA Ops:
  0.6 59.4 %shard_map.67 = (f32[4,128]{1,0:T(4,128)S(1)}, bf16[64,256]{1,0:T(8,128)(2,1)S(1)}, bf16[1024,4096]{1,0:T(8,128)(2,1)S(1)}) custom-call(bf16[64,256]{1,0:T(8,128)(2,1)} %hid_ref.1, bf16[1024,4096]{1,0:T(8,128)(2,1)} %w_hbm.1, s32[1,512]{1,0:T(1,128)} %bitcast.3, f32[1,512]{1,0:T(1,128)} %bitcast.4), custom_call_target="tpu_custom_call" | custom-call | tf_op jit(solution)/shard_map/pallas_call | solution.py:365
  60.1 3.4 %shard_map.68 = (bf16[1024,4096]{1,0:T(8,128)(2,1)}, f32[4,128]{1,0:T(4,128)}, bf16[64,256]{1,0:T(8,128)(2,1)}) custom-call(bf16[1024,4096]{1,0:T(8,128)(2,1)S(1)} %get-tuple-element.9.gw, f32[4,128]{1,0:T(4,128)S(1)} %get-tuple-element.10.loss, bf16[64,256]{1,0:T(8,128)(2,1)S(1)} %get-tuple-element.11.gh), custom_call_target="tpu_custom_call" | custom-call | tf_op jit(solution)/shard_map/pallas_call | solution.py:395

commit v4 on v3

--- a/solution.py
+++ b/solution.py
@@ -12,7 +12,7 @@
 ORDERS = ((X, Y, Z), (Y, Z, X), (X, Z, Y))
 ROWS = ((0, 32), (32, 48), (80, 48))
 NEAR = (1, 3, 2)
-COPIES = 191
+COPIES = 188
 PIECES = 8
 
 
@@ -48,12 +48,12 @@
 
 
 def kernel(
-    hid_ref, w_hbm, tgt_ref, lg_ref,
+    hid_hbm, w_hbm, tgt_hbm, lg_hbm,
     loss_ref, gh_ref, gw_ref,
     w, g, lt, glt, gl, own, give, take, r,
     a0, b0, c0, a1, b1, c1, fa, fb, fc,
-    st_plane, st_axis,
-    w_sem, send_sem, recv_sem,
+    st_core, st_plane, st_axis,
+    tgt_ref, lg_ref, local_sem, send_sem, recv_sem,
 ):
     x, y, z, c = place()
     me = (x, y, z)
@@ -61,27 +61,37 @@
     tokens = lt.shape[1]
     partner = device(x, y, z, 1 - c)
 
-    def there(moves, cc=c):
-        return device(*[(me[a] + moves.get(a, 0)) % 4 for a in range(3)], cc)
-
-    load_w = pltpu.make_async_copy(w_hbm, w, w_sem)
-    load_w.start()
-
-    own_g = (c,) + region(me)
-    g[own_g + (pl.ds(0, 64),)] = hid_ref[:, 0:128]
-    g[own_g + (pl.ds(64, 64),)] = hid_ref[:, 128:256]
+    def settle(upto=None):
+        upto = len(copies) if upto is None else upto
+        for cp in copies[len(settled) : upto]:
+            cp.wait_send()
+            settled.append(cp)
+
+    def there(moves):
+        return device(*[(me[a] + moves.get(a, 0)) % 4 for a in range(3)], c)
 
     barrier = pltpu.get_barrier_semaphore()
     peers = [partner]
     for d in NEAR:
-        peers += [there({axis: d}) for axis in (X, Y, Z)] + [there({Z: d}, 1 - c)]
+        peers += [there({axis: d}) for axis in (X, Y, Z)]
         peers += [there({p: d, q: e}) for p, q in ((X, Y), (Y, Z), (X, Z)) for e in NEAR]
     for to in peers:
         pl.semaphore_signal(barrier, inc=1, device_id=to, device_id_type=MESH)
+    own_g = (c,) + region(me)
+    pairs = [
+        (hid_hbm.at[:, pl.ds(0, 128)], g.at[own_g + (pl.ds(0, 64),)]),
+        (hid_hbm.at[:, pl.ds(128, 128)], g.at[own_g + (pl.ds(64, 64),)]),
+        (tgt_hbm, tgt_ref), (lg_hbm, lg_ref), (w_hbm, w),
+    ]
+    loads = [pltpu.make_async_copy(a, b, local_sem.at[i]) for i, (a, b) in enumerate(pairs)]
+    for cp in loads:
+        cp.start()
     lt[...] = jnp.zeros_like(lt)
+    for cp in loads[:4]:
+        cp.wait()
     pl.semaphore_wait(barrier, len(peers))
 
-    copies = []
+    copies, settled = [], []
 
     def send(src, dst, to):
         i = len(copies)
@@ -159,7 +169,7 @@
             cp.wait_recv()
 
     relayed = {0: relay(0)}
-    load_w.wait()
+    loads[4].wait()
     arrived(relayed[0])
     logits(0)
     for s in NEAR:
@@ -201,23 +211,24 @@
 
     for j, v in enumerate((top, total, picked)):
         for i in range(4):
-            st_plane[0, j, i : i + 1, :] = v[:, 128 * i : 128 * (i + 1)]
+            st_core[0, j, i : i + 1, :] = v[:, 128 * i : 128 * (i + 1)]
+    gathered = len(copies)
+    send(st_core.at[0], st_core.at[1], partner).wait_recv()
+    for j, v in enumerate(combine(st_core[...])):
+        st_plane[0, j] = v
     joined = []
     for dx in range(4):
         for dy in range(4):
             i = dx * 4 + dy
             if i:
                 joined.append(send(st_plane.at[0], st_plane.at[i], there({X: dx, Y: dy})))
+    settle(gathered)
     for cp in joined:
         cp.wait_recv()
     for j, v in enumerate(combine(st_plane[...])):
         st_axis[0, j] = v
-    joined = [
-        send(st_axis.at[0], st_axis.at[d * 2 + i], there({Z: d}, cc))
-        for i, cc in enumerate((c, 1 - c))
-        for d in (0,) + NEAR
-        if d or i
-    ]
+    joined = [send(st_axis.at[0], st_axis.at[d], there({Z: d})) for d in NEAR]
+    settle(len(copies) - len(joined))
     for cp in joined:
         cp.wait_recv()
     m_all, s_all, p_all = combine(st_axis[...])
@@ -310,6 +321,7 @@
             r[:, :, (z + s) % 4, xx] = (own[xx] + take[i, xx].astype(F32)).astype(BF16)
         reduce_z(s)
     weight_grad(0, 1)
+    reduced = len(copies)
     for k in (1, 2):
         pass_line(k, 1)
     weight_grad(1, 2)
@@ -326,6 +338,7 @@
     for k in (1, 2):
         pass_line(k, 0)
     weight_grad(3, 4)
+    settle(reduced)
     mine = region(me)
     for k in range(3):
         axis = ORDERS[k][0]
@@ -340,8 +353,7 @@
     gh_ref[:, 128:256] = r[mine + (pl.ds(64, 64),)]
 
     assert len(copies) == COPIES, len(copies)
-    for cp in copies:
-        cp.wait_send()
+    settle()
 
 
 def write_kernel(gw, loss, gh, gw_out, loss_out, gh_out, sem):
@@ -369,7 +381,7 @@
             pltpu.VMEM(hidden.shape, BF16),
             pltpu.VMEM((vocab, depth), BF16),
         ),
-        in_specs=[vmem, anywhere, vmem, vmem],
+        in_specs=[anywhere] * 4,
         out_specs=(vmem, vmem, vmem),
         scratch_shapes=[
             pltpu.VMEM((vocab, depth), BF16),
@@ -384,9 +396,12 @@
             slot(3, 2, 4, 2, 32), slot(4, 3, 4, 48), slot(4, 3, 2, 2, 48),
             slot(16, 32), slot(16, 48), slot(16, 48),
             slot(2, 2, 32, t=F32), slot(4, 48, t=F32), slot(2, 2, 48, t=F32),
+            pltpu.VMEM((2, 3, 4, 128), F32),
             pltpu.VMEM((16, 3, 4, 128), F32),
-            pltpu.VMEM((8, 3, 4, 128), F32),
-            dma, dma((COPIES,)), dma((COPIES,)),
+            pltpu.VMEM((4, 3, 4, 128), F32),
+            pltpu.VMEM((1, tokens), jnp.int32),
+            pltpu.VMEM((1, tokens), F32),
+            dma((5,)), dma((COPIES,)), dma((COPIES,)),
         ],
         compiler_params=pltpu.CompilerParams(
             collective_id=0, has_side_effects=True, vmem_limit_bytes=48 * 2**20

time: 63.8 us -> 62.9 us (0.986)
  Pallas kernels: 62.8 us -> 61.8 us
    pallas_call x1, Pallas kernels: 59.4 us -> 58.4 us  [shards(): pl.pallas_call(kernel, out_shape=(pltpu.VMEM((4, 128), F32), pltpu.VMEM(h...]
where the time goes in v4:
time: 62.9 us; the launch traced here: 62.6 us
  Pallas kernels  61.8 us (98%)
  between operations  0.8 us (1%)
    pallas_call x1, Pallas kernels, shards(): pl.pallas_call(kernel, out_shape=(pltpu.VMEM((4, 128), F32), pltpu.VMEM(h...  58.4 us
    pallas_call x1, Pallas kernels, shards(): pl.pallas_call(write_kernel, out_shape=(jax.ShapeDtypeStruct((vocab, dept...  3.39 us

profile of v4, /device:TPU:0, one launch (start us, length us, event | category | flops | bytes accessed | tf_op | source)
XLA Modules:
  0.0 62.6 jit_solution(10337985054706484456)
XLA Ops:
  0.6 58.4 %shard_map.67 = (f32[4,128]{1,0:T(4,128)S(1)}, bf16[64,256]{1,0:T(8,128)(2,1)S(1)}, bf16[1024,4096]{1,0:T(8,128)(2,1)S(1)}) custom-call(bf16[64,256]{1,0:T(8,128)(2,1)} %hid_hbm.1, bf16[1024,4096]{1,0:T(8,128)(2,1)} %w_hbm.1, s32[1,512]{1,0:T(1,128)} %bitcast.3, f32[1,512]{1,0:T(1,128)} %bitcast.4), custom_call_target="tpu_custom_call" | custom-call | tf_op jit(solution)/shard_map/pallas_call | solution.py:377
  59.1 3.4 %shard_map.68 = (bf16[1024,4096]{1,0:T(8,128)(2,1)}, f32[4,128]{1,0:T(4,128)}, bf16[64,256]{1,0:T(8,128)(2,1)}) custom-call(bf16[1024,4096]{1,0:T(8,128)(2,1)S(1)} %get-tuple-element.9.gw, f32[4,128]{1,0:T(4,128)S(1)} %get-tuple-element.10.loss, bf16[64,256]{1,0:T(8,128)(2,1)S(1)} %get-tuple-element.11.gh), custom_call_target="tpu_custom_call" | custom-call | tf_op jit(solution)/shard_map/pallas_call | solution.py:410

commit v5 on v4

--- a/solution.py
+++ b/solution.py
@@ -12,7 +12,7 @@
 ORDERS = ((X, Y, Z), (Y, Z, X), (X, Z, Y))
 ROWS = ((0, 32), (32, 48), (80, 48))
 NEAR = (1, 3, 2)
-COPIES = 188
+COPIES = 185
 PIECES = 8
 
 
@@ -124,15 +124,16 @@
             for d in (0,) + NEAR:
                 if s or d:
                     got1[k, s, d].wait_recv()
-            for d in NEAR:
+            for d in NEAR if k else (1, 3):
                 got2[k, s, d] = spread(k, there({ORDERS[k][2]: d}), first="all", second=-s)
+    got2[0, 0, 2] = spread(0, there({Z: 2}), first="all", second="all")
 
     def relay(s):
         done = []
         for k in range(3):
             if k == 0:
                 if s:
-                    for i in (0,) + NEAR:
+                    for i in (0,) if s == 2 else (0,) + NEAR:
                         got2[0, i, s].wait_recv()
             else:
                 for d in NEAR:
@@ -234,11 +235,11 @@
     m_all, s_all, p_all = combine(st_axis[...])
     loss_ref[...] = m_all + jnp.log(s_all) - p_all
     lg = lg_ref[...]
-    scale = lg * jnp.exp(top - flat(m_all)) / flat(s_all)
+    scale = jnp.exp(top - flat(m_all)) / flat(s_all)
 
     def grad_step(i, _):
         rows = pl.ds(pl.multiple_of(i * chunk, chunk), chunk)
-        value = lt[rows, :] * scale - jnp.where(hit(i), lg, 0.0)
+        value = lg * (lt[rows, :] * scale - jnp.where(hit(i), 1.0, 0.0))
         glt[rows, :] = value.astype(BF16)
         return 0
 

time: 62.9 us -> 63 us (level)
  no operation moved by 1% of the time
where the time goes in v5:
time: 63 us; the launch traced here: 62.7 us
  Pallas kernels  61.9 us (98%)
  between operations  0.8 us (1%)
    pallas_call x1, Pallas kernels, shards(): pl.pallas_call(kernel, out_shape=(pltpu.VMEM((4, 128), F32), pltpu.VMEM(h...  58.5 us
    pallas_call x1, Pallas kernels, shards(): pl.pallas_call(write_kernel, out_shape=(jax.ShapeDtypeStruct((vocab, dept...  3.39 us

profile of v5, /device:TPU:0, one launch (start us, length us, event | category | flops | bytes accessed | tf_op | source)
XLA Modules:
  0.0 62.7 jit_solution(14872191963855828534)
XLA Ops:
  0.6 58.5 %shard_map.67 = (f32[4,128]{1,0:T(4,128)S(1)}, bf16[64,256]{1,0:T(8,128)(2,1)S(1)}, bf16[1024,4096]{1,0:T(8,128)(2,1)S(1)}) custom-call(bf16[64,256]{1,0:T(8,128)(2,1)} %hid_hbm.1, bf16[1024,4096]{1,0:T(8,128)(2,1)} %w_hbm.1, s32[1,512]{1,0:T(1,128)} %bitcast.3, f32[1,512]{1,0:T(1,128)} %bitcast.4), custom_call_target="tpu_custom_call" | custom-call | tf_op jit(solution)/shard_map/pallas_call | solution.py:378
  59.1 3.4 %shard_map.68 = (bf16[1024,4096]{1,0:T(8,128)(2,1)}, f32[4,128]{1,0:T(4,128)}, bf16[64,256]{1,0:T(8,128)(2,1)}) custom-call(bf16[1024,4096]{1,0:T(8,128)(2,1)S(1)} %get-tuple-element.9.gw, f32[4,128]{1,0:T(4,128)S(1)} %get-tuple-element.10.loss, bf16[64,256]{1,0:T(8,128)(2,1)S(1)} %get-tuple-element.11.gh), custom_call_target="tpu_custom_call" | custom-call | tf_op jit(solution)/shard_map/pallas_call | solution.py:411

commit v6 on v4

--- a/solution.py
+++ b/solution.py
@@ -184,7 +184,7 @@
 
     s_idx, t_idx = lax.axis_index("section"), lax.axis_index("tensor")
     local = tgt_ref[...] - (s_idx * 16 + t_idx) * vocab
-    chunk = 64
+    chunk = 128
     n_chunks = vocab // chunk
 
     def hit(i):
@@ -272,8 +272,8 @@
         if s:
             ref = r.at[region(spot(0, first="all", second="all", last=s), ROWS[0])]
             red0[0, s] = send(ref, a0.at[s - 1], there({Z: s}))
-        for k in (1, 2):
-            for d in NEAR:
+        for d in NEAR:
+            for k in (1, 2):
                 ref = r.at[region(spot(k, first="all", second=s, last=d), ROWS[k])]
                 red0[k, s, d] = send(ref, slots0[k].at[s, d - 1], there({ORDERS[k][2]: d}))
 

time: 62.9 us -> 62.8 us (level)
  no operation moved by 1% of the time
where the time goes in v6:
time: 62.8 us; the launch traced here: 62.5 us
  Pallas kernels  61.7 us (98%)
  between operations  0.8 us (1%)
    pallas_call x1, Pallas kernels, shards(): pl.pallas_call(kernel, out_shape=(pltpu.VMEM((4, 128), F32), pltpu.VMEM(h...  58.4 us
    pallas_call x1, Pallas kernels, shards(): pl.pallas_call(write_kernel, out_shape=(jax.ShapeDtypeStruct((vocab, dept...  3.39 us

profile of v6, /device:TPU:0, one launch (start us, length us, event | category | flops | bytes accessed | tf_op | source)
XLA Modules:
  0.0 62.5 jit_solution(411681925297198342)
XLA Ops:
  0.6 58.4 %shard_map.67 = (f32[4,128]{1,0:T(4,128)S(1)}, bf16[64,256]{1,0:T(8,128)(2,1)S(1)}, bf16[1024,4096]{1,0:T(8,128)(2,1)S(1)}) custom-call(bf16[64,256]{1,0:T(8,128)(2,1)} %hid_hbm.1, bf16[1024,4096]{1,0:T(8,128)(2,1)} %w_hbm.1, s32[1,512]{1,0:T(1,128)} %bitcast.3, f32[1,512]{1,0:T(1,128)} %bitcast.4), custom_call_target="tpu_custom_call" | custom-call | tf_op jit(solution)/shard_map/pallas_call | solution.py:377
  59.0 3.4 %shard_map.68 = (bf16[1024,4096]{1,0:T(8,128)(2,1)}, f32[4,128]{1,0:T(4,128)}, bf16[64,256]{1,0:T(8,128)(2,1)}) custom-call(bf16[1024,4096]{1,0:T(8,128)(2,1)S(1)} %get-tuple-element.9.gw, f32[4,128]{1,0:T(4,128)S(1)} %get-tuple-element.10.loss, bf16[64,256]{1,0:T(8,128)(2,1)S(1)} %get-tuple-element.11.gh), custom_call_target="tpu_custom_call" | custom-call | tf_op jit(solution)/shard_map/pallas_call | solution.py:410
